TPU v7x, 512 devices: a whole 4x8x8 slice. The times are simulated.
512 devices in a mesh: grp: 32 (over y_lo, z, core), seq: 16 (over x, y_hi).
Axes of the slice: x: 4, y: 8 (y_hi: 4, y_lo: 2; y = y_hi * 2 + y_lo), z: 8, core: 2. Of those that a mesh axis runs over, the one named last changes fastest.
Arguments:
- query: bfloat16 [131072, 1280], P(('grp', 'seq')), may hold values from -64 to 64
- keys: bfloat16 [131072, 1280], P(('grp', 'seq')), may hold values from -4 to 4
- values: bfloat16 [131072, 1280], P(('grp', 'seq')), may hold values from -5 to 5
- cotangent: bfloat16 [131072, 1280], P(('grp', 'seq')), may hold values from -5 to 5
Outputs:
- attended: bfloat16 [131072, 1280], P(('grp', 'seq'))
- query_grad: bfloat16 [131072, 1280], P(('grp', 'seq'))
- key_grad: bfloat16 [131072, 1280], P(('grp', 'seq'))
- value_grad: bfloat16 [131072, 1280], P(('grp', 'seq'))
All inputs are finite; a program needn't handle non-finite values.
Results may differ from a plain program's by a relative error of at most 0.022.
Values may be sent and summed in bfloat16 or wider, within the bound.
A program may use at most 128 MiB of HBM per device.

v0:
```python
import math

import jax
import jax.numpy as jnp
from jax import lax
from jax.sharding import PartitionSpec as P

HEADS = 16
POOL = 16


SCORE_FLOOR = -1e30


def shifted(block, axis, distance):
    devices = range(lax.axis_size(axis))
    route = [(i - distance, i) for i in devices if i - distance in devices]
    return lax.ppermute(block, axis, route)


def split_heads(matrix, heads):
    return matrix.reshape(matrix.shape[0], heads, matrix.shape[1] // heads)


def head_slice(matrix, index, group_heads):
    return lax.dynamic_slice_in_dim(matrix, index * group_heads, group_heads, 1)


def pooled(matrix, width):
    summed = matrix.astype(jnp.float32).reshape(-1, width, matrix.shape[1]).sum(axis=1)
    return (summed / math.sqrt(width)).astype(jnp.bfloat16)


def visibility(block, member, rows, n_seq, coarse, devices):
    group = block // n_seq
    row_ids = jnp.arange(rows, dtype=jnp.int32)[:, None]
    col_ids = jnp.arange(rows, dtype=jnp.int32)[None, :]
    before = jnp.broadcast_to(block > 0, (rows, rows))
    inside = col_ids <= row_ids
    owner = jnp.arange(n_seq * coarse, dtype=jnp.int32) // coarse
    middle = jnp.broadcast_to((owner < member)[None, :], (rows, n_seq * coarse))
    far_ids = jnp.arange(devices, dtype=jnp.int32)
    distant = jnp.broadcast_to(
        (far_ids < jnp.minimum(group * n_seq, block - 1))[None, :], (rows, devices)
    )
    return jnp.concatenate([before, inside, middle, distant], axis=1)


def forward_block(query, keys_all, values_all, visible, heads):
    group_heads = 2
    rows = query.shape[0]
    scale = 1.0 / math.sqrt(query.shape[1] // heads)
    query_h = split_heads(query, heads)
    keys_h = split_heads(keys_all, heads)
    values_h = split_heads(values_all, heads)

    def forward_one_group(index):
        query_g = head_slice(query_h, index, group_heads)
        keys_g = head_slice(keys_h, index, group_heads)
        values_g = head_slice(values_h, index, group_heads)
        scores = (
            jnp.einsum("qhe,khe->hqk", query_g, keys_g, preferred_element_type=jnp.float32) * scale
        )
        scores = jnp.where(visible[None], scores, SCORE_FLOOR)
        top = jnp.max(scores, axis=2, keepdims=True)
        expo = jnp.exp(scores - top)
        total = jnp.sum(expo, axis=2, keepdims=True)
        weights = (expo / total).astype(jnp.bfloat16)
        mixed = jnp.einsum("hqk,khe->qhe", weights, values_g, preferred_element_type=jnp.float32)
        return (mixed, (top + jnp.log(total))[:, :, 0])

    mixed, lse = lax.map(forward_one_group, jnp.arange(heads // group_heads, dtype=jnp.int32))
    attended = jnp.moveaxis(mixed, 0, 1).reshape(rows, -1).astype(jnp.bfloat16)
    return (attended, lse.reshape(heads, rows))


def head_products(cotangent, attended, heads):
    rows = cotangent.shape[0]
    product = cotangent.astype(jnp.float32) * attended.astype(jnp.float32)
    return product.reshape(rows, heads, -1).sum(axis=2).T


def backward_block(query, keys_all, values_all, visible, cotangent, lse, delta, heads):
    group_heads = 2
    rows = query.shape[0]
    scale = 1.0 / math.sqrt(query.shape[1] // heads)
    query_h = split_heads(query, heads)
    keys_h = split_heads(keys_all, heads)
    values_h = split_heads(values_all, heads)
    cot_h = split_heads(cotangent, heads)

    def backward_one_group(index):
        query_g = head_slice(query_h, index, group_heads)
        keys_g = head_slice(keys_h, index, group_heads)
        values_g = head_slice(values_h, index, group_heads)
        cot_g = head_slice(cot_h, index, group_heads)
        lse_g = lax.dynamic_slice_in_dim(lse, index * group_heads, group_heads, 0)
        delta_g = lax.dynamic_slice_in_dim(delta, index * group_heads, group_heads, 0)
        scores = (
            jnp.einsum("qhe,khe->hqk", query_g, keys_g, preferred_element_type=jnp.float32) * scale
        )
        scores = jnp.where(visible[None], scores, SCORE_FLOOR)
        probs = jnp.exp(scores - lse_g[:, :, None])
        dprob = jnp.einsum("qhe,khe->hqk", cot_g, values_g, preferred_element_type=jnp.float32)
        dscore = (probs * (dprob - delta_g[:, :, None])).astype(jnp.bfloat16)
        weights = probs.astype(jnp.bfloat16)
        query_part = (
            jnp.einsum("hqk,khe->qhe", dscore, keys_g, preferred_element_type=jnp.float32) * scale
        )
        key_part = (
            jnp.einsum("hqk,qhe->khe", dscore, query_g, preferred_element_type=jnp.float32) * scale
        )
        value_part = jnp.einsum("hqk,qhe->khe", weights, cot_g, preferred_element_type=jnp.float32)
        return (query_part, key_part, value_part)

    query_part, key_part, value_part = lax.map(
        backward_one_group, jnp.arange(heads // group_heads, dtype=jnp.int32)
    )
    query_grad = jnp.moveaxis(query_part, 0, 1).reshape(rows, -1)
    key_grad = jnp.moveaxis(key_part, 0, 1).reshape(key_part.shape[1], -1)
    value_grad = jnp.moveaxis(value_part, 0, 1).reshape(value_part.shape[1], -1)
    return (query_grad, key_grad, value_grad)


def body(query, keys, values, cotangent):
    rows = query.shape[0]
    n_seq = lax.axis_size("seq")
    devices = lax.axis_size("grp") * n_seq
    group = lax.axis_index("grp")
    member = lax.axis_index("seq")
    block = group * n_seq + member
    coarse = rows // POOL
    group_rows = n_seq * coarse
    local_mid_k = pooled(keys, POOL)
    local_mid_v = pooled(values, POOL)
    mid_k, mid_v = (
        lax.all_gather(local_mid_k, "seq", axis=0, tiled=True),
        lax.all_gather(local_mid_v, "seq", axis=0, tiled=True),
    )
    far_k, far_v = (
        lax.all_gather(pooled(mid_k, coarse), "grp", axis=0, tiled=True),
        lax.all_gather(pooled(mid_v, coarse), "grp", axis=0, tiled=True),
    )
    prev_k, prev_v = shifted((keys, values), ("grp", "seq"), 1)
    keys_all = jnp.concatenate([prev_k, keys, mid_k, far_k], axis=0)
    values_all = jnp.concatenate([prev_v, values, mid_v, far_v], axis=0)
    visible = visibility(block, member, rows, n_seq, coarse, devices)
    attended, lse = forward_block(query, keys_all, values_all, visible, HEADS)
    delta = head_products(cotangent, attended, HEADS)
    query_grad, key_grad, value_grad = backward_block(
        query, keys_all, values_all, visible, cotangent, lse, delta, HEADS
    )
    back_k, back_v = (
        shifted(key_grad[:rows].astype(jnp.bfloat16), ("grp", "seq"), -1).astype(jnp.float32),
        shifted(value_grad[:rows].astype(jnp.bfloat16), ("grp", "seq"), -1).astype(jnp.float32),
    )
    fine_k = key_grad[rows : 2 * rows] + back_k
    fine_v = value_grad[rows : 2 * rows] + back_v
    rest_k = key_grad[2 * rows :]
    rest_v = value_grad[2 * rows :]
    part_k = rest_k.astype(jnp.bfloat16)
    part_v = rest_v.astype(jnp.bfloat16)
    far_sum_k, far_sum_v = (
        lax.psum_scatter(part_k[group_rows:], "grp", scatter_dimension=0, tiled=True).astype(
            jnp.float32
        ),
        lax.psum_scatter(part_v[group_rows:], "grp", scatter_dimension=0, tiled=True).astype(
            jnp.float32
        ),
    )
    own_far_k, own_far_v = (
        lax.psum_scatter(
            far_sum_k.astype(jnp.bfloat16), "seq", scatter_dimension=0, tiled=True
        ).astype(jnp.float32),
        lax.psum_scatter(
            far_sum_v.astype(jnp.bfloat16), "seq", scatter_dimension=0, tiled=True
        ).astype(jnp.float32),
    )
    own_mid_k, own_mid_v = (
        lax.psum_scatter(part_k[:group_rows], "seq", scatter_dimension=0, tiled=True).astype(
            jnp.float32
        ),
        lax.psum_scatter(part_v[:group_rows], "seq", scatter_dimension=0, tiled=True).astype(
            jnp.float32
        ),
    )
    spread_k = (own_mid_k + own_far_k / math.sqrt(coarse)) / math.sqrt(POOL)
    spread_v = (own_mid_v + own_far_v / math.sqrt(coarse)) / math.sqrt(POOL)
    key_out = (fine_k + jnp.repeat(spread_k, POOL, axis=0)).astype(jnp.bfloat16)
    value_out = (fine_v + jnp.repeat(spread_v, POOL, axis=0)).astype(jnp.bfloat16)
    return (attended, query_grad.astype(jnp.bfloat16), key_out, value_out)


def solution(mesh):
    in_specs = (
        P(("grp", "seq"), None),
        P(("grp", "seq"), None),
        P(("grp", "seq"), None),
        P(("grp", "seq"), None),
    )
    out_specs = (
        P(("grp", "seq"), None),
        P(("grp", "seq"), None),
        P(("grp", "seq"), None),
        P(("grp", "seq"), None),
    )
    return jax.shard_map(body, mesh=mesh, in_specs=in_specs, out_specs=out_specs, check_vma=False)
```

profile of v0, /device:TPU:6, one launch (start us, length us, event | category | flops | bytes accessed | tf_op | source)
XLA Modules:
  0.0 984.7 jit_solution(16472955342818412634)
XLA Ops:
  8.7 43.3 %all_gather.14 = bf16[256,1280]{1,0:T(8,128)(2,1)S(1)} all-gather(bf16[16,1280]{1,0:T(8,128)(2,1)S(1)} %multiply_convert_fusion.1), channel_id=1, replica_groups=mesh['grp'=32,'seq'=16] {'seq'}, dimensions={0}, use_global_device_ids=true | all-gather | bytes 696320 | tf_op jit(solution)/shard_map/all_gather | solution.py:137
  54.2 67.5 %all_gather.12 = bf16[256,1280]{1,0:T(8,128)(2,1)S(1)} all-gather(bf16[16,1280]{1,0:T(8,128)(2,1)S(1)} %multiply_convert_fusion.3), channel_id=1, replica_groups=mesh['grp'=32,'seq'=16] {'seq'}, dimensions={0}, use_global_device_ids=true | all-gather | bytes 696320 | tf_op jit(solution)/shard_map/all_gather | solution.py:138
  130.5 14.0 %collective-permute-done.1 = bf16[256,1280]{1,0:T(8,128)(2,1)S(1)} collective-permute-done((bf16[256,1280]{1,0:T(8,128)(2,1)S(1)}, bf16[256,1280]{1,0:T(8,128)(2,1)S(1)}, u32[]{:S(2)}, u32[]{:S(2)}) %collective-permute-start.1) | collective-permute-done | bytes 655392 | tf_op jit(solution)/shard_map/ppermute | solution.py:18
  144.6 2.9 pad_maximum_fusion.1
  147.5 4.0 copy.56
  151.7 62.3 %all-gather.3.cloned.1.call-done = bf16[512,1280]{1,0:T(8,128)(2,1)} async-done(((bf16[16,1280]{1,0:T(8,128)(2,1)}), bf16[512,1280]{1,0:T(8,128)(2,1)}) %all-gather.3.cloned.1.call-update) | async-done | bytes 1310736 | tf_op jit(solution)/shard_map/all_gather | solution.py:142
  214.0 3.2 pad_maximum_fusion
  217.2 5.7 copy.54
  223.7 48.3 %while.26 = (s32[]{:T(128)}, bf16[8,256,2,80]{1,3,2,0:T(8,128)(2,1)}, f32[8,2,256]{2,1,0:T(2,128)S(1)}, s32[8]{0:T(128)S(1)}, bf16[1280,16,80]{0,2,1:T(8,128)(2,...) while((s32[]{:T(128)}, ...), condition=%wide.region_7.8_spmd, body=%wide.region_4.7_spmd.sunk | while | flops 214957568 | bytes 9275063 | solution.py:72
  227.4 2.4 fusion.69
  233.4 2.4 fusion.69
  239.4 2.4 fusion.69
  245.5 2.4 fusion.69
  251.5 2.4 fusion.69
  257.5 2.4 fusion.69
  263.6 2.4 fusion.69
  269.6 2.4 fusion.69
  272.0 2.5 convert_multiply_fusion
  276.8 83.1 %while.27 = (s32[]{:T(128)}, bf16[8,256,2,80]{1,3,2,0:T(8,128)(2,1)}, f32[8,1280,2,80]{1,3,2,0:T(8,128)}, f32[8,1280,2,80]{1,3,2,0:T(8,128)}, s32[8]{0:T(128)S(1...) while((s32[]{:T(128)}, ...), condition=%wide.region_10.11_spmd, body=%wide.region_9.10_spmd.sunk | while | flops 529121280 | bytes 15498975 | solution.py:116
  283.9 2.2 fusion.84
  292.1 2.2 fusion.83
  302.5 2.2 fusion.83
  304.7 2.2 fusion.84
  312.9 2.1 fusion.83
  315.1 2.2 fusion.84
  323.3 2.1 fusion.83
  333.7 2.1 fusion.83
  335.8 2.2 fusion.84
  344.1 2.2 fusion.83
  346.2 2.2 fusion.84
  354.5 2.2 fusion.83
  356.6 2.2 fusion.84
  360.0 5.4 bitcast_convert_fusion
  368.3 2.4 copy.63
  372.0 2.4 copy.60
  374.5 116.0 %reduce-scatter.11.cloned.1.call-done = bf16[16,1280]{1,0:T(8,128)(2,1)} async-done(((bf16[512,1280]{1,0:T(8,128)(2,1)}), bf16[16,1280]{1,0:T(8,128)(2,1)}) %reduce-scatter.11.cloned.1.call-update) | async-done | bytes 40976 | tf_op jit(solution)/shard_map/reduce_scatter | solution.py:167
  490.5 118.6 %reduce-scatter.7.cloned.1.call-done = bf16[16,1280]{1,0:T(8,128)(2,1)} async-done(((bf16[512,1280]{1,0:T(8,128)(2,1)}), bf16[16,1280]{1,0:T(8,128)(2,1)}) %reduce-scatter.7.cloned.1.call-update) | async-done | bytes 40976 | tf_op jit(solution)/shard_map/reduce_scatter | solution.py:164
  609.2 2.4 fusion.43
  611.7 2.2 copy.62
  615.1 2.3 copy.59
  617.4 5.0 collective-permute-start.3
  623.7 2.5 slice.74
  626.2 4.8 collective-permute-start.2
  632.5 2.2 copy.66
  634.6 2.2 copy.65
  636.8 146.4 %all-reduce.5.cloned.1.call-done = (bf16[16,1280]{1,0:T(8,128)(2,1)}, bf16[16,1280]{1,0:T(8,128)(2,1)}) async-done(((bf16[16,1280]{1,0:T(8,128)(2,1)}, bf16[16,1280]{1,0:T(8,128)(2,1)}), (bf16[16,1280]{1,0:T(8,128)(2,1)}, bf16[16,1280]{1,0:T(8,128)(2,1)})) %all-reduce.5.cloned.1.call-update) | async-done | bytes 81936
  784.6 94.1 %reduce-scatter.9.cloned.1.call-done = bf16[16,1280]{1,0:T(8,128)(2,1)} async-done(((bf16[256,1280]{1,0:T(8,128)(2,1)}), bf16[16,1280]{1,0:T(8,128)(2,1)}) %reduce-scatter.9.cloned.1.call-update) | async-done | bytes 40976 | tf_op jit(solution)/shard_map/reduce_scatter | solution.py:183
  885.6 87.1 %reduce-scatter.5.cloned.1.call-done = bf16[16,1280]{1,0:T(8,128)(2,1)} async-done(((bf16[256,1280]{1,0:T(8,128)(2,1)}), bf16[16,1280]{1,0:T(8,128)(2,1)}) %reduce-scatter.5.cloned.1.call-update) | async-done | bytes 40976 | tf_op jit(solution)/shard_map/reduce_scatter | solution.py:180
  (151 shorter events, 110.4 us)
Async XLA Ops:
  7.2 116.3 %copy-start.2 = (bf16[256,1280]{1,0:T(8,128)(2,1)S(1)}, bf16[256,1280]{1,0:T(8,128)(2,1)}, u32[]{:S(2)}) copy-start(bf16[256,1280]{1,0:T(8,128)(2,1)} %param.9) | copy-start | bytes 1966084
  7.2 120.3 %copy-start.4 = (bf16[256,1280]{1,0:T(8,128)(2,1)S(1)}, bf16[256,1280]{1,0:T(8,128)(2,1)}, u32[]{:S(2)}) copy-start(bf16[256,1280]{1,0:T(8,128)(2,1)} %param.8) | copy-start | bytes 1966084
  7.2 137.4 %all-gather.5.cloned.1.call-start = ((), (), s32[]{:S(2)}) async-start(), calls=%async_computation.5 | async-start | bytes 1351680 | tf_op jit(solution)/shard_map/all_gather | solution.py:141
  8.6 119.9 %copy-start.5 = (bf16[256,1280]{1,0:T(8,128)(2,1)S(1)}, bf16[256,1280]{1,0:T(8,128)(2,1)}, u32[]{:S(2)}) copy-start(bf16[256,1280]{1,0:T(8,128)(2,1)} %param.11) | copy-start | bytes 1966084
  52.8 161.2 %all-gather.3.cloned.1.call-start = ((), (), s32[]{:S(2)}) async-start(), calls=%async_computation.4 | async-start | bytes 1351680 | tf_op jit(solution)/shard_map/all_gather | solution.py:142
  121.7 0.8 copy-start.1
  123.4 367.1 %reduce-scatter.11.cloned.1.call-start = ((), (), s32[]{:S(2)}) async-start(), calls=%async_computation.9 | async-start | bytes 1351680 | tf_op jit(solution)/shard_map/reduce_scatter | solution.py:167
  123.5 21.1 %collective-permute-start.1 = (bf16[256,1280]{1,0:T(8,128)(2,1)S(1)}, bf16[256,1280]{1,0:T(8,128)(2,1)S(1)}, u32[]{:S(2)}, u32[]{:S(2)}) collective-permute-start(bf16[256,1280]{1,0:T(8,128)(2,1)S(1)} %copy-done.2), channel_id=1, source_target_pairs={{0,1},{1,2},{2,3},{3,4},{4,5},{5,6},{6,7},{7,8},{8,9},{9,10},{10,1... | collective-permute-start | bytes 1966088 | tf_op jit(solution)/shard_map/ppermute | solution.py:18
  125.4 26.3 %collective-permute-start = (bf16[256,1280]{1,0:T(8,128)(2,1)}, bf16[256,1280]{1,0:T(8,128)(2,1)}, u32[]{:S(2)}, u32[]{:S(2)}) collective-permute-start(bf16[256,1280]{1,0:T(8,128)(2,1)} %param.10), channel_id=1, source_target_pairs={{0,1},{1,2},{2,3},{3,4},{4,5},{5,6},{6,7},{7,8},{8,9},{9,10},{10,1... | collective-permute-start | bytes 1966088 | tf_op jit(solution)/shard_map/ppermute | solution.py:18
  365.4 1.7 copy-start
  370.7 238.4 %reduce-scatter.7.cloned.1.call-start = ((), (), s32[]{:S(2)}) async-start(), calls=%async_computation.7 | async-start | bytes 1351680 | tf_op jit(solution)/shard_map/reduce_scatter | solution.py:164
  374.5 408.7 %all-reduce.5.cloned.1.call-start = ((), (), s32[]{:S(2)}) async-start(), calls=%async_computation.10 | async-start | bytes 163840
  609.2 269.5 %reduce-scatter.9.cloned.1.call-start = ((), (), s32[]{:S(2)}) async-start(), calls=%async_computation.8 | async-start | bytes 696320 | tf_op jit(solution)/shard_map/reduce_scatter | solution.py:183
  613.9 358.8 %reduce-scatter.5.cloned.1.call-start = ((), (), s32[]{:S(2)}) async-start(), calls=%async_computation.6 | async-start | bytes 696320 | tf_op jit(solution)/shard_map/reduce_scatter | solution.py:180
  615.1 11.1 %copy-start.3 = (bf16[256,8,2,80]{0,3,2,1:T(8,128)(2,1)S(1)}, bf16[256,8,2,80]{0,3,2,1:T(8,128)(2,1)}, u32[]{:S(2)}) copy-start(bf16[256,8,2,80]{0,3,2,1:T(8,128)(2,1)} %get-tuple-element.196) | copy-start | bytes 1966084
  617.4 263.6 %collective-permute-start.3 = (bf16[256,1280]{0,1:T(8,128)(2,1)}, bf16[256,1280]{0,1:T(8,128)(2,1)}, u32[]{:S(2)}, u32[]{:S(2)}) collective-permute-start(bf16[256,1280]{0,1:T(8,128)(2,1)} %bitcast.112), channel_id=1, source_target_pairs={{1,0},{2,1},{3,2},{4,3},{5,4},{6,5},{7,6},{8,7},{9,8},{10,9},{11,1... | collective-permute-start | bytes 1966088 | tf_op jit(solution)/shard_map/ppermute | solution.py:18
  626.2 348.8 %collective-permute-start.2 = (bf16[256,1280]{0,1:T(8,128)(2,1)S(1)}, bf16[256,1280]{0,1:T(8,128)(2,1)}, u32[]{:S(2)}, u32[]{:S(2)}) collective-permute-start(bf16[256,1280]{0,1:T(8,128)(2,1)S(1)} %bitcast.111), channel_id=1, source_target_pairs={{1,0},{2,1},{3,2},{4,3},{5,4},{6,5},{7,6},{8,7},{9,8},{10,9},{11,1... | collective-permute-start | bytes 1966088 | tf_op jit(solution)/shard_map/ppermute | solution.py:18
Sparse Core Ops, SparseCore 0:
  52.9 91.5 all-gather.4
  147.3 66.6 all-gather.2
  370.9 119.6 reduce-scatter.10
  493.4 115.6 reduce-scatter.6
  612.0 171.1 all-reduce.4
  787.6 90.9 reduce-scatter.8
  883.2 89.3 reduce-scatter.4
where the time goes:
time: 988 us; the launch traced here: 985 us
  waiting for transfers between devices  639 us (65%)
  blocking collectives  111 us (11%)
  matrix products  106 us (11%)
  local copies, waits for them, and re-layouts  56.4 us (6%)
  other arithmetic  33.5 us (3%)
  between operations  14.4 us (1%)
  starting transfers between devices  13.9 us (1%)
  loops' own time  11.1 us (1%)
    unnamed x8, waiting for transfers between devices  146 us
    reduce_scatter x1, waiting for transfers between devices, body(): lax.psum_scatter(part_k[group_rows:], 'grp', scatter_dimension=0, tiled=T...  119 us
    reduce_scatter x1, waiting for transfers between devices, body(): lax.psum_scatter(part_v[group_rows:], 'grp', scatter_dimension=0, tiled=T...  116 us
    reduce_scatter x1, waiting for transfers between devices, body(): lax.psum_scatter(part_v[:group_rows], 'seq', scatter_dimension=0, tiled=T...  94.1 us
    reduce_scatter x1, waiting for transfers between devices, body(): lax.psum_scatter(part_k[:group_rows], 'seq', scatter_dimension=0, tiled=T...  87.1 us
    all_gather x1, blocking collectives, body(): lax.all_gather(local_mid_v, 'seq', axis=0, tiled=True)  67.5 us
    all_gather x1, waiting for transfers between devices, body(): lax.all_gather(pooled(mid_v, coarse), 'grp', axis=0, tiled=True)  62.3 us
    all_gather x1, blocking collectives, body(): lax.all_gather(local_mid_k, 'seq', axis=0, tiled=True)  43.3 us
  transfers between devices with their start and end apart: 11, of which 8 were waited for; matrix products, arithmetic and copies ran while one was open for 4% of the time, Pallas kernels for 0%

commit v1 on v0

v1 whole, which is shorter than its diff:
```python
import functools
import math

import jax
import jax.numpy as jnp
from jax import lax
from jax.experimental import pallas as pl
from jax.experimental.pallas import tpu as pltpu
from jax.sharding import PartitionSpec as P

HEADS = 16
POOL = 16
HALVES = 2
TILE = 128
WINDOW = 256
PAIR = 2
FLOOR = -1e30
LOG2E = 1.4426950408889634
MESH = pl.DeviceIdType.MESH
F32 = jnp.float32
BF16 = jnp.bfloat16


def dot(a, b):
    return jnp.dot(a, b, preferred_element_type=F32)


def kernel(
    n_grp, n_seq,
    q_hbm, k_hbm, v_hbm, c_hbm,
    o_hbm, dq_hbm, dk_hbm, dv_hbm,
    kv, qc, qn, kvt, qc_t, bias, score, weight, dscore,
    out_t, dq_t, out_rows, stat, stat_next, own, mid_part, far_part,
    core_in, core_sum, far_in, far_rows, far_rows_in,
    mid_x_in, mid_x, mid_y_in, grad_rows, far_mine, far_all, padded,
    load_sem, row_send, row_recv, y_send, y_recv, key_send, key_recv, query_send, query_recv, x_send, x_recv, z_send, z_recv,
    pair_send, pair_recv, stat_send, stat_recv, core_send, core_recv,
    mx_send, mx_recv, my_send, my_recv, fz_send, fz_recv, fs_send, fs_recv, store_sem,
):
    rows = q_hbm.shape[0]
    width = q_hbm.shape[1]
    part = width // HALVES
    heads = HEADS // HALVES
    depth = width // HEADS
    coarse = rows // POOL
    mid_rows = n_seq * coarse
    n_far = n_grp * n_seq
    half = n_far // 2
    y_n = math.isqrt(n_seq)
    x_n = n_seq // y_n
    z_n = n_grp // 2
    mid_at = 2 * rows
    far_at = mid_at + mid_rows
    scale = 1.0 / math.sqrt(depth)
    to_log2 = scale * LOG2E
    tiles = part // TILE

    g = lax.axis_index("grp")
    m = lax.axis_index("seq")
    core = g % 2
    zz = g // 2
    xx = m // y_n
    yy = m % y_n
    block = g * n_seq + m
    n_blocks = n_grp * n_seq
    after = (block + 1) % n_blocks
    before = (block + n_blocks - 1) % n_blocks
    next_id = (after // n_seq, after % n_seq)
    prev_id = (before // n_seq, before % n_seq)
    twin_id = (2 * zz + 1 - core, m)

    def y_peer(d):
        return (yy + d) % y_n

    def x_peer(d):
        return (xx + d) % x_n

    def z_peer(i):
        return (zz + i) % z_n

    def remote(src, dst, send, recv, device):
        return pltpu.make_async_remote_copy(
            src_ref=src, dst_ref=dst, send_sem=send, recv_sem=recv,
            device_id=device, device_id_type=MESH,
        )

    def aligned(start, unit):
        return pl.multiple_of(start, unit)

    loads = []
    for c in range(HALVES):
        cols = pl.ds(c * part, part)
        for kind, (ref, dst) in enumerate((
            (k_hbm, kv.at[c, 0, pl.ds(rows, rows)]), (v_hbm, kv.at[c, 1, pl.ds(rows, rows)]),
            (q_hbm, qc.at[c, 0]), (c_hbm, qc.at[c, 1]),
        )):
            loads.append(pltpu.make_async_copy(ref.at[:, cols], dst, load_sem.at[c * 4 + kind]))
    for copy in loads:
        copy.start()

    barrier = pltpu.get_barrier_semaphore()

    def greet(device):
        pl.semaphore_signal(barrier, inc=1, device_id=device, device_id_type=MESH)

    def greet_seq(i, carry):
        greet((g, (m + i) % n_seq))
        return carry

    def greet_z(i, carry):
        greet((2 * z_peer(i) + core, m))
        return carry

    lax.fori_loop(1, n_seq, greet_seq, 0)
    lax.fori_loop(1, z_n, greet_z, 0)
    greet(twin_id)
    greet(next_id)
    greet(prev_id)

    for c in range(HALVES):
        for kind in range(2):
            loads[c * 4 + kind].wait()

    def pooling(n, count):
        row = lax.broadcasted_iota(jnp.int32, (n, n * count), 0)
        col = lax.broadcasted_iota(jnp.int32, (n, n * count), 1)
        return jnp.where((col >= row * count) & (col < row * count + count), 1.0, 0.0).astype(BF16)

    own_mid = pl.ds(aligned(mid_at + m * coarse, coarse), coarse)
    pool_mid = pooling(coarse, POOL)
    for c in range(HALVES):
        for kind in range(2):
            summed = dot(pool_mid, kv[c, kind, rows : 2 * rows, :])
            pooled = (summed / math.sqrt(POOL)).astype(BF16)
            kv[c, kind, own_mid, :] = pooled
            row = jnp.sum(pooled.astype(F32), axis=0, keepdims=True) / math.sqrt(coarse)
            row = row.astype(BF16).astype(F32)
            for t in range(tiles):
                at = c * 16 + kind * 8 + t
                far_mine[at : at + 1, :] = row[:, t * TILE : (t + 1) * TILE]

    pl.semaphore_wait(barrier, (n_seq - 1) + (z_n - 1) + 3)

    def row_copy(i, source, device):
        spot = far_all.at[pl.ds(aligned(source * 32, 32), 32), :]
        return remote(far_mine, spot, row_send.at[i], row_recv.at[i], device)

    def send_row(i, carry):
        row_copy(i, m, (g, (m + i) % n_seq)).start()
        return carry

    lax.fori_loop(1, n_seq, send_row, 0)
    far_all[pl.ds(aligned(m * 32, 32), 32), :] = far_mine[...]

    def mid_slot(member_start, count):
        return pl.ds(aligned(mid_at + member_start * coarse, coarse), count * coarse)

    y_copies = []
    for d in range(1, y_n):
        spot = kv.at[:, :, own_mid, :]
        copy = remote(spot, spot, y_send.at[d], y_recv.at[d], (g, xx * y_n + y_peer(d)))
        copy.start()
        y_copies.append(copy)

    def key_copy(c, t):
        cols = pl.ds(aligned(t * TILE, TILE), TILE)
        return remote(kv.at[c, :, pl.ds(rows, rows), cols], kv.at[c, :, pl.ds(0, rows), cols],
                      key_send.at[c, t], key_recv.at[c, t], next_id)

    def query_copy(c, t):
        cols = pl.ds(aligned(t * TILE, TILE), TILE)
        return remote(qc.at[c, :, :, cols], qn.at[c, :, :, cols],
                      query_send.at[c, t], query_recv.at[c, t], prev_id)

    for copy in loads[2:4] + loads[6:8]:
        copy.wait()

    def start_raw(c, first, last):
        for t in range(first, last):
            key_copy(c, t).start()
            query_copy(c, t).start()

    start_raw(0, 0, 2)

    def fill_constants():
        for c in range(HALVES):
            own[c] = jnp.zeros(own.shape[1:], F32)
            mid_part[c] = jnp.zeros(mid_part.shape[1:], BF16)
            far_part[c] = jnp.zeros(far_part.shape[1:], BF16)
        bias[0:rows, :] = jnp.full((rows, rows), jnp.where(block > 0, 0.0, FLOOR), F32)
        key_row = lax.broadcasted_iota(jnp.int32, (rows, rows), 0)
        query_col = lax.broadcasted_iota(jnp.int32, (rows, rows), 1)
        bias[rows : 2 * rows, :] = jnp.where(key_row <= query_col, 0.0, FLOOR)
        mid_row = lax.broadcasted_iota(jnp.int32, (mid_rows, rows), 0)
        bias[mid_at : mid_at + mid_rows, :] = jnp.where(mid_row < m * coarse, 0.0, FLOOR)
        far_row = lax.broadcasted_iota(jnp.int32, (half, rows), 0)
        limit = jnp.minimum(g * n_seq, block - 1)
        for side in range(2):
            far_block = (2 * (far_row // n_seq) + side) * n_seq + far_row % n_seq
            at = far_at + side * half
            bias[at : at + half, :] = jnp.where(far_block < limit, 0.0, FLOOR)

    def far_slot(which):
        return pl.ds(aligned(far_at + core * half + which * n_seq, n_seq), n_seq)

    def far_copy(c, i, which, device):
        spot = kv.at[c, :, far_slot(which), :]
        return remote(spot, spot, z_send.at[c, i], z_recv.at[c, i], device)

    def start_far(c):
        def send(i, carry):
            far_copy(c, i, zz, (2 * z_peer(i) + core, m)).start()
            return carry

        lax.fori_loop(1, z_n, send, 0)

    def row_arrived(i, carry):
        row_copy(i, (m + n_seq - i) % n_seq, (g, m)).wait_recv()
        return carry

    lax.fori_loop(1, n_seq, row_arrived, 0)
    for c in range(HALVES):
        for kind in range(2):
            for t in range(tiles):
                lines = far_all[pl.ds(c * 16 + kind * 8 + t, n_seq, stride=32), :]
                kv[c, kind, far_slot(zz), t * TILE : (t + 1) * TILE] = lines.astype(BF16)
    start_far(0)

    for d in range(1, y_n):
        source = mid_slot(xx * y_n + (yy + y_n - d) % y_n, 1)
        spot = kv.at[:, :, source, :]
        remote(spot, spot, y_send.at[d], y_recv.at[d], (g, m)).wait_recv()
    x_copies = []
    for c in range(HALVES):
        for d in range(1, x_n):
            spot = kv.at[c, :, mid_slot(xx * y_n, y_n), :]
            copy = remote(spot, spot, x_send.at[c, d], x_recv.at[c, d], (g, x_peer(d) * y_n + yy))
            copy.start()
            x_copies.append(copy)
    start_raw(0, 2, tiles)
    fill_constants()

    def mid_ready(c):
        for d in range(1, x_n):
            spot = kv.at[c, :, mid_slot((xx + x_n - d) % x_n * y_n, y_n), :]
            remote(spot, spot, x_send.at[c, d], x_recv.at[c, d], (g, m)).wait_recv()

    def pair_copy(c):
        spot = kv.at[c, :, pl.ds(aligned(far_at + core * half, half), half), :]
        return remote(spot, spot, pair_send.at[c], pair_recv.at[c], twin_id)

    def forward_far(c):
        def arrived(i, carry):
            far_copy(c, i, (zz + z_n - i) % z_n, (g, m)).wait_recv()
            return carry

        lax.fori_loop(1, z_n, arrived, 0)
        pair_copy(c).start()

    def far_ready(c):
        spot = kv.at[c, :, pl.ds(aligned(far_at + (1 - core) * half, half), half), :]
        remote(spot, spot, pair_send.at[c], pair_recv.at[c], (g, m)).wait_recv()

    total = far_at + n_far

    def head_window(j):
        tile = jnp.maximum((j * depth + depth - 1) // TILE - 1, 0)
        start = aligned(tile * TILE, TILE)
        lane = lax.broadcasted_iota(jnp.int32, (8, WINDOW), 1) + start
        inside = (lane >= j * depth) & (lane < j * depth + depth)
        keep = jnp.where(inside, 1.0, 0.0)[0:1, :]
        return pl.ds(start, WINDOW), keep, j * depth - start

    def only(loaded, keep):
        return (loaded.astype(F32) * keep).astype(BF16)

    def pad_head(u, j, kind, offset):
        padded[u, kind] = jnp.zeros((WINDOW, rows), BF16)
        padded[u, kind, pl.ds(aligned(offset, 16), depth), :] = qc_t[
            kind, pl.ds(aligned(j * depth, depth), depth), :
        ]
        return padded[u, kind]

    def main(c):
        for kind in range(2):
            kvt[kind, :, rows:total] = kv[c, kind, rows:total, :].T
            qc_t[kind] = qc[c, kind].T

        def arrive(t):
            key_copy(c, t).wait_recv()
            cols = pl.ds(aligned(t * TILE, TILE), TILE)
            for kind in range(2):
                kvt[kind, cols, 0:rows] = kv[c, kind, 0:rows, cols].T

        arrive(0)

        def step(i, carry):
            if c == 0:
                @pl.when(i == 2)
                def _():
                    forward_far(1)
            else:
                @pl.when(i == 1)
                def _():
                    send_far(0, 1)

            @pl.when(i == 2)
            def _():
                core_copy(c, 0).start()

            @pl.when(i == 3)
            def _():
                send_far(c, 0)

            arrive(i + 1)
            js = [i * PAIR + u for u in range(PAIR)]
            windows, queries, cots, cots_t, tops = [], [], [], [], []
            for u, j in enumerate(js):
                window, keep, offset = head_window(j)
                windows.append(window)
                queries.append(only(qc[c, 0, :, window], keep))
                cots.append(only(qc[c, 1, :, window], keep))
                cots_t.append(pad_head(u, j, 1, offset))
                s = dot(kv[c, 0, :, window], pad_head(u, j, 0, offset)) + bias[...]
                score[u] = s
                tops.append(jnp.max(s, axis=0, keepdims=True) * to_log2)
            inverses, deltas = [], []
            for u, j in enumerate(js):
                e = jnp.exp2(score[u] * to_log2 - tops[u])
                score[u] = e
                norm = jnp.sum(e, axis=0, keepdims=True)
                inverse = 1.0 / norm
                weight[u] = (score[u] * inverse).astype(BF16)
                inverses.append(inverse)
                head_rows = pl.ds(aligned(j * depth, depth), depth)
                mixed = dot(kvt[1, head_rows, :], weight[u]).astype(BF16)
                out_t[head_rows, :] = mixed
                delta = jnp.sum(
                    qc_t[1, head_rows, :].astype(F32) * mixed.astype(F32), axis=0, keepdims=True
                )
                deltas.append(delta)
                stat[c, pl.ds(j, 1), :] = tops[u] + jnp.log(norm) * LOG2E
                stat[c, pl.ds(heads + j, 1), :] = delta
            for u, j in enumerate(js):
                dprob = dot(kv[c, 1, :, windows[u]], cots_t[u])
                dscore[u] = (score[u] * ((dprob - deltas[u]) * inverses[u])).astype(BF16)
                head_rows = pl.ds(aligned(j * depth, depth), depth)
                dq_t[head_rows, :] = (dot(kvt[0, head_rows, :], dscore[u]) * scale).astype(BF16)
                for kind, (left, right) in enumerate(((dscore, queries[u]), (weight, cots[u]))):
                    grad = dot(left[u, rows:total, :], right)
                    own[c, kind, :, windows[u]] += grad[0:rows]
                    mid_part[c, kind, :, windows[u]] += grad[rows : rows + mid_rows].astype(BF16)
                    far_part[c, kind, :, windows[u]] += grad[rows + mid_rows :].astype(BF16)
            return carry

        lax.fori_loop(0, heads // PAIR, step, 0)

    def stat_copy(c):
        return remote(stat.at[c], stat_next.at[c], stat_send.at[c], stat_recv.at[c], prev_id)

    def store(c, kind, src, ref):
        return pltpu.make_async_copy(src, ref.at[:, pl.ds(c * part, part)], store_sem.at[c * 4 + kind])

    def piece(p):
        return pl.ds(0, 2 * TILE) if p == 0 else pl.ds(2 * TILE, part - 2 * TILE)

    def core_copy(c, p):
        src = far_part.at[c, :, pl.ds(aligned((1 - core) * half, half), half), piece(p)]
        return remote(src, core_in.at[c, :, :, piece(p)], core_send.at[c, p], core_recv.at[c, p], twin_id)

    def mid_x_copy(c, d):
        src = mid_part.at[c, :, pl.ds(aligned(x_peer(d) * y_n * coarse, coarse), y_n * coarse), :]
        return remote(src, mid_x_in.at[c, d - 1], mx_send.at[c, d], mx_recv.at[c, d],
                      (g, x_peer(d) * y_n + yy))

    def mid_y_copy(c, d):
        src = mid_x.at[c, :, pl.ds(aligned(y_peer(d) * coarse, coarse), coarse), :]
        return remote(src, mid_y_in.at[c, d - 1], my_send.at[c, d], my_recv.at[c, d],
                      (g, xx * y_n + y_peer(d)))

    def far_z_copy(c, p, i):
        src = core_sum.at[c, :, pl.ds(aligned(z_peer(i) * n_seq, n_seq), n_seq), piece(p)]
        return remote(src, far_in.at[c, i, :, :, piece(p)], fz_send.at[c, p, i], fz_recv.at[c, p, i],
                      (2 * z_peer(i) + core, m))

    def far_row_copy(c, i):
        member = (m + i) % n_seq
        src = far_rows.at[c, pl.ds(aligned(member * 16, 16), 16), :]
        dst = far_rows_in.at[c, pl.ds(aligned(i * 16, 16), 16), :]
        return remote(src, dst, fs_send.at[c, i], fs_recv.at[c, i], (g, member))

    def send_parts(c):
        core_copy(c, 1).start()
        stat_copy(c).start()
        for d in range(1, x_n):
            mid_x_copy(c, d).start()
        out_rows[c, 0] = out_t[...].T
        out_rows[c, 1] = dq_t[...].T
        store(c, 0, out_rows.at[c, 0], o_hbm).start()
        store(c, 1, out_rows.at[c, 1], dq_hbm).start()

    def send_far(c, p):
        core_copy(c, p).wait_recv()
        mine = pl.ds(aligned(core * half, half), half)
        for kind in range(2):
            both = far_part[c, kind, mine, piece(p)].astype(F32) + core_in[c, kind, :, piece(p)].astype(F32)
            core_sum[c, kind, :, piece(p)] = both.astype(BF16)

        def send(i, carry):
            far_z_copy(c, p, i).start()
            return carry

        lax.fori_loop(1, z_n, send, 0)

    def send_mid(c):
        for d in range(1, x_n):
            mid_x_copy(c, d).wait_recv()
        mine = pl.ds(aligned(xx * y_n * coarse, coarse), y_n * coarse)
        for kind in range(2):
            added = mid_part[c, kind, mine, :].astype(F32)
            for d in range(1, x_n):
                added = added + mid_x_in[c, d - 1, kind].astype(F32)
            mid_x[c, kind] = added.astype(BF16)
        for d in range(1, y_n):
            mid_y_copy(c, d).start()

    def send_rows(c):
        def arrived(i, carry):
            far_z_copy(c, 0, i).wait_recv()
            far_z_copy(c, 1, i).wait_recv()
            return carry

        lax.fori_loop(1, z_n, arrived, 0)
        mine = pl.ds(aligned(zz * n_seq, n_seq), n_seq)
        for kind in range(2):
            def add(i, added, kind=kind):
                return added + far_in[c, i, kind].astype(F32)

            added = lax.fori_loop(1, z_n, add, core_sum[c, kind, mine, :].astype(F32))
            for t in range(tiles):
                far_rows[c, pl.ds(kind * 8 + t, n_seq, stride=16), :] = added[:, t * TILE : (t + 1) * TILE]

        def send(i, carry):
            far_row_copy(c, i).start()
            return carry

        lax.fori_loop(1, n_seq, send, 0)
        far_rows_in[c, 0:16, :] = far_rows[c, pl.ds(aligned(m * 16, 16), 16), :]

    def from_next(c):
        for t in range(tiles):
            query_copy(c, t).wait_recv()
        stat_copy(c).wait_recv()
        for kind in range(2):
            qc_t[kind] = qn[c, kind].T
        there = block < n_blocks - 1

        def step(i, carry):
            for u in range(PAIR):
                j = i * PAIR + u
                window, keep, offset = head_window(j)
                query = only(qn[c, 0, :, window], keep)
                cot = only(qn[c, 1, :, window], keep)
                s = dot(kv[c, 0, rows : 2 * rows, window], pad_head(u, j, 0, offset))
                s = jnp.where(there, s, FLOOR)
                p = jnp.exp2(s * to_log2 - stat_next[c, pl.ds(j, 1), :])
                dprob = dot(kv[c, 1, rows : 2 * rows, window], pad_head(u, j, 1, offset))
                ds = (p * (dprob - stat_next[c, pl.ds(heads + j, 1), :])).astype(BF16)
                own[c, 0, :, window] += dot(ds, query)
                own[c, 1, :, window] += dot(p.astype(BF16), cot)
            return carry

        lax.fori_loop(0, heads // PAIR, step, 0)

    def finish(c):
        for d in range(1, y_n):
            mid_y_copy(c, d).wait_recv()

        def arrived(i, carry):
            far_row_copy(c, i).wait_recv()
            return carry

        lax.fori_loop(1, n_seq, arrived, 0)
        far_sum = far_rows_in[c, 0:16, :]
        for i in range(1, n_seq):
            far_sum = far_sum + far_rows_in[c, i * 16 : (i + 1) * 16, :]
        mine = pl.ds(aligned(yy * coarse, coarse), coarse)
        for kind in range(2):
            factor = scale if kind == 0 else 1.0
            added = mid_x[c, kind, mine, :].astype(F32)
            for d in range(1, y_n):
                added = added + mid_y_in[c, d - 1, kind].astype(F32)
            for t in range(tiles):
                cols = slice(t * TILE, (t + 1) * TILE)
                far = far_sum[kind * 8 + t : kind * 8 + t + 1, :] / math.sqrt(coarse)
                spread = (added[:, cols] + far) * (factor / math.sqrt(POOL))
                for i in range(coarse):
                    raw = own[c, kind, i * POOL : (i + 1) * POOL, cols] * factor
                    grad_rows[c, kind, i * POOL : (i + 1) * POOL, cols] = (
                        raw + spread[i : i + 1, :]
                    ).astype(BF16)
        store(c, 2, grad_rows.at[c, 0], dk_hbm).start()
        store(c, 3, grad_rows.at[c, 1], dv_hbm).start()

    forward_far(0)
    start_far(1)
    start_raw(1, 0, tiles)
    mid_ready(0)
    far_ready(0)
    main(0)
    send_parts(0)
    mid_ready(1)
    far_ready(1)
    main(1)
    send_parts(1)
    send_mid(0)
    send_far(1, 1)
    from_next(0)
    send_rows(0)
    send_mid(1)
    from_next(1)
    finish(0)
    send_rows(1)
    finish(1)

    for copy in y_copies + x_copies:
        copy.wait_send()
    for c in range(HALVES):
        for t in range(tiles):
            key_copy(c, t).wait_send()
            query_copy(c, t).wait_send()
        pair_copy(c).wait_send()
        stat_copy(c).wait_send()
        core_copy(c, 0).wait_send()
        core_copy(c, 1).wait_send()
        for d in range(1, x_n):
            mid_x_copy(c, d).wait_send()
        for d in range(1, y_n):
            mid_y_copy(c, d).wait_send()

        def left_z(i, carry, c=c):
            far_copy(c, i, zz, (2 * z_peer(i) + core, m)).wait_send()
            far_z_copy(c, 0, i).wait_send()
            far_z_copy(c, 1, i).wait_send()
            return carry

        def left_rows(i, carry, c=c):
            far_row_copy(c, i).wait_send()
            if c == 0:
                row_copy(i, m, (g, (m + i) % n_seq)).wait_send()
            return carry

        lax.fori_loop(1, z_n, left_z, 0)
        lax.fori_loop(1, n_seq, left_rows, 0)
        store(c, 0, out_rows.at[c, 0], o_hbm).wait()
        store(c, 1, out_rows.at[c, 1], dq_hbm).wait()
        store(c, 2, grad_rows.at[c, 0], dk_hbm).wait()
        store(c, 3, grad_rows.at[c, 1], dv_hbm).wait()


def hand_over(a, b, c, d, to_a, to_b, to_c, to_d):
    for src, dst in ((a, to_a), (b, to_b), (c, to_c), (d, to_d)):
        dst[...] = src[...]


def body(query, keys, values, cotangent):
    rows, width = query.shape
    n_seq = lax.axis_size("seq")
    n_grp = lax.axis_size("grp")
    part = width // HALVES
    coarse = rows // POOL
    mid_rows = n_seq * coarse
    n_far = n_grp * n_seq
    half = n_far // 2
    total = 2 * rows + mid_rows + n_far
    y_n = math.isqrt(n_seq)
    x_n = n_seq // y_n
    z_n = n_grp // 2
    heads = HEADS // HALVES
    tiles = part // TILE
    vmem = pltpu.VMEM
    dma = pltpu.SemaphoreType.DMA
    scratch = [
        vmem((HALVES, 2, total, part), BF16),
        vmem((HALVES, 2, rows, part), BF16),
        vmem((HALVES, 2, rows, part), BF16),
        vmem((2, part, total), BF16),
        vmem((2, part, rows), BF16),
        vmem((total, rows), F32),
        vmem((PAIR, total, rows), F32),
        vmem((PAIR, total, rows), BF16),
        vmem((PAIR, total, rows), BF16),
        vmem((part, rows), BF16),
        vmem((part, rows), BF16),
        vmem((HALVES, 2, rows, part), BF16),
        vmem((HALVES, 2 * heads, rows), F32),
        vmem((HALVES, 2 * heads, rows), F32),
        vmem((HALVES, 2, rows, part), F32),
        vmem((HALVES, 2, mid_rows, part), BF16),
        vmem((HALVES, 2, n_far, part), BF16),
        vmem((HALVES, 2, half, part), BF16),
        vmem((HALVES, 2, half, part), BF16),
        vmem((HALVES, z_n, 2, n_seq, part), BF16),
        vmem((HALVES, n_seq * 16, TILE), F32),
        vmem((HALVES, n_seq * 16, TILE), F32),
        vmem((HALVES, x_n - 1, 2, y_n * coarse, part), BF16),
        vmem((HALVES, 2, y_n * coarse, part), BF16),
        vmem((HALVES, y_n - 1, 2, coarse, part), BF16),
        vmem((HALVES, 2, rows, part), BF16),
        vmem((32, TILE), F32),
        vmem((n_seq * 32, TILE), F32),
        vmem((PAIR, 2, WINDOW, rows), BF16),
        dma((HALVES * 4,)),
        dma((n_seq,)), dma((n_seq,)),
        dma((y_n,)), dma((y_n,)),
        dma((HALVES, tiles)), dma((HALVES, tiles)),
        dma((HALVES, tiles)), dma((HALVES, tiles)),
        dma((HALVES, x_n)), dma((HALVES, x_n)),
        dma((HALVES, z_n)), dma((HALVES, z_n)),
        dma((HALVES,)), dma((HALVES,)),
        dma((HALVES,)), dma((HALVES,)),
        dma((HALVES, 2)), dma((HALVES, 2)),
        dma((HALVES, x_n)), dma((HALVES, x_n)),
        dma((HALVES, y_n)), dma((HALVES, y_n)),
        dma((HALVES, 2, z_n)), dma((HALVES, 2, z_n)),
        dma((HALVES, n_seq)), dma((HALVES, n_seq)),
        dma((HALVES * 4,)),
    ]
    flops = 12 * rows * total * width
    results = pl.pallas_call(
        functools.partial(kernel, n_grp, n_seq),
        out_shape=[jax.ShapeDtypeStruct((rows, width), BF16)] * 4,
        in_specs=[pl.BlockSpec(memory_space=pl.ANY)] * 4,
        out_specs=[pl.BlockSpec(memory_space=pl.ANY)] * 4,
        scratch_shapes=scratch,
        compiler_params=pltpu.CompilerParams(
            collective_id=0, has_side_effects=True, vmem_limit_bytes=60 * 2**20
        ),
        cost_estimate=pl.CostEstimate(
            flops=flops, bytes_accessed=16 * rows * width, transcendentals=HEADS * rows * total
        ),
    )(query, keys, values, cotangent)
    block = pl.BlockSpec((rows // 4, width), lambda i: (i, 0))
    return pl.pallas_call(
        hand_over,
        grid=(4,),
        out_shape=[jax.ShapeDtypeStruct((rows, width), BF16)] * 4,
        in_specs=[block] * 4,
        out_specs=[block] * 4,
        cost_estimate=pl.CostEstimate(flops=0, bytes_accessed=16 * rows * width, transcendentals=0),
        compiler_params=pltpu.CompilerParams(vmem_limit_bytes=60 * 2**20),
    )(*results)


def solution(mesh):
    spec = P(("grp", "seq"), None)
    return jax.shard_map(
        body, mesh=mesh, in_specs=(spec,) * 4, out_specs=(spec,) * 4, check_vma=False
    )
```

time: 988 us -> 146 us (0.15)
  waiting for transfers between devices: 639 us -> 0 us
  Pallas kernels: 0 us -> 144 us
  blocking collectives: 111 us -> 0 us
  matrix products: 106 us -> 0 us
  local copies, waits for them, and re-layouts: 56.4 us -> 0 us
  other arithmetic: 33.5 us -> 0 us
  starting transfers between devices: 13.9 us -> 0 us
  between operations: 14.4 us -> 0.64 us
  loops' own time: 11.1 us -> 0 us
    reduce_scatter x4 -> x0, waiting for transfers between devices: 416 us -> none  [the longest x1 119 us: body(): lax.psum_scatter(part_k[group_rows:], 'grp', scatter_dimension=0, tiled=T...]
    unnamed x8 -> x0, waiting for transfers between devices: 146 us -> none
    pallas_call x0 -> x2, Pallas kernels: none -> 144 us  [the longest x1 140 us: body(): pl.pallas_call(functools.partial(kernel, n_grp, n_seq), out_shape=[jax.Sh...]
    all_gather x2 -> x0, blocking collectives: 111 us -> none  [the longest x1 67.5 us: body(): lax.all_gather(local_mid_v, 'seq', axis=0, tiled=True)]
    dot_general x56 -> x0, matrix products: 106 us -> none  [the longest x8 19.2 us: forward_one_group(): jnp.einsum('hqk,khe->qhe', weights, values_g, preferred_element_type=jnp....]
    all_gather x2 -> x0, waiting for transfers between devices: 62.3 us -> none  [the longest x1 62.3 us: body(): lax.all_gather(pooled(mid_v, coarse), 'grp', axis=0, tiled=True)]
    slice x10 -> x0, local copies, waits for them, and re-layouts: 19.3 us -> none  [the longest x2 3.64 us: body(): part_v[group_rows:]]
    ppermute x4 -> x0, waiting for transfers between devices: 14.1 us -> none  [shifted(): return lax.ppermute(block, axis, route)]
  transfers between devices with their start and end apart: 11 -> 0, of which waited for: 8 -> 0; matrix products, arithmetic and copies ran while one was open for 4% -> 0% of each run, Pallas kernels for 0% -> 0%
where the time goes in v1:
time: 146 us; the launch traced here: 144 us
  Pallas kernels  144 us (99%)
    pallas_call x1, Pallas kernels, body(): pl.pallas_call(functools.partial(kernel, n_grp, n_seq), out_shape=[jax.Sh...  140 us
    pallas_call x1, Pallas kernels, body(): pl.pallas_call(hand_over, grid=(4,), out_shape=[jax.ShapeDtypeStruct((row...  4.02 us

profile of v1, /device:TPU:6, one launch (start us, length us, event | category | flops | bytes accessed | tf_op | source)
XLA Modules:
  0.0 144.3 jit_solution(13054071389801631580)
XLA Ops:
  0.6 139.7 %shard_map.75 = (bf16[256,1280]{1,0:T(8,128)(2,1)}, bf16[256,1280]{1,0:T(8,128)(2,1)}, bf16[256,1280]{1,0:T(8,128)(2,1)}, bf16[256,1280]{1,0:T(8,128)(2,1)}) custom-call(bf16[256,1280]{1,0:T(8,128)(2,1)} %q_hbm.1, bf16[256,1280]{1,0:T(8,128)(2,1)} %k_hbm.1, bf16[256,1280]{1,0:T(8,128)(2,1)} %v_hbm.1, bf16[256,1280]{1,0:T(8,128)(2,1)} %c_hbm.1), custom_call_target="tpu_custom_call" | custom-call | flops 5033164800 | bytes 5242880 | tf_op jit(solution)/shard_map/pallas_call | solution.py:630
  140.3 4.0 %shard_map.76 = (bf16[256,1280]{1,0:T(8,128)(2,1)}, bf16[256,1280]{1,0:T(8,128)(2,1)}, bf16[256,1280]{1,0:T(8,128)(2,1)}, bf16[256,1280]{1,0:T(8,128)(2,1)}) custom-call(bf16[256,1280]{1,0:T(8,128)(2,1)} %get-tuple-element.8.a, bf16[256,1280]{1,0:T(8,128)(2,1)} %get-tuple-element.9.b, bf16[256,1280]{1,0:T(8,128)(2,1)} %get-tuple-element.10.c, ...), custom_call_target="tpu_custom_call" | custom-call | bytes 5242880 | tf_op jit(solution)/shard_map/pallas_call | solution.py:644

commit v2 on v1

--- a/solution.py
+++ b/solution.py
@@ -32,8 +32,8 @@
     kv, qc, qn, kvt, qc_t, bias, score, weight, dscore,
     out_t, dq_t, out_rows, stat, stat_next, own, mid_part, far_part,
     core_in, core_sum, far_in, far_rows, far_rows_in,
-    mid_x_in, mid_x, mid_y_in, grad_rows, far_mine, far_all, padded,
-    load_sem, row_send, row_recv, y_send, y_recv, key_send, key_recv, query_send, query_recv, x_send, x_recv, z_send, z_recv,
+    mid_x_in, mid_x, mid_y_in, grad_rows, far_mine, far_all, padded, cross_out, cross_in, z_sum, mine_z,
+    load_sem, across_send, across_recv, cross_send, cross_recv, row_send, row_recv, y_send, y_recv, key_send, key_recv, query_send, query_recv, x_send, x_recv, z_send, z_recv,
     pair_send, pair_recv, stat_send, stat_recv, core_send, core_recv,
     mx_send, mx_recv, my_send, my_recv, fz_send, fz_recv, fs_send, fs_recv, store_sem,
 ):
@@ -48,7 +48,7 @@
     half = n_far // 2
     y_n = math.isqrt(n_seq)
     x_n = n_seq // y_n
-    z_n = n_grp // 2
+    z_n = n_grp // 4
     mid_at = 2 * rows
     far_at = mid_at + mid_rows
     scale = 1.0 / math.sqrt(depth)
@@ -58,7 +58,8 @@
     g = lax.axis_index("grp")
     m = lax.axis_index("seq")
     core = g % 2
-    zz = g // 2
+    side_y = g // 2 // z_n
+    zz = g // 2 % z_n
     xx = m // y_n
     yy = m % y_n
     block = g * n_seq + m
@@ -67,7 +68,8 @@
     before = (block + n_blocks - 1) % n_blocks
     next_id = (after // n_seq, after % n_seq)
     prev_id = (before // n_seq, before % n_seq)
-    twin_id = (2 * zz + 1 - core, m)
+    twin_id = (g + 1 - 2 * core, m)
+    across_id = (2 * ((1 - side_y) * z_n + zz) + core, m)
 
     def y_peer(d):
         return (yy + d) % y_n
@@ -77,6 +79,9 @@
 
     def z_peer(i):
         return (zz + i) % z_n
+
+    def z_id(i):
+        return (2 * (side_y * z_n + z_peer(i)) + core, m)
 
     def remote(src, dst, send, recv, device):
         return pltpu.make_async_remote_copy(
@@ -108,12 +113,13 @@
         return carry
 
     def greet_z(i, carry):
-        greet((2 * z_peer(i) + core, m))
+        greet(z_id(i))
         return carry
 
     lax.fori_loop(1, n_seq, greet_seq, 0)
     lax.fori_loop(1, z_n, greet_z, 0)
     greet(twin_id)
+    greet(across_id)
     greet(next_id)
     greet(prev_id)
 
@@ -139,7 +145,7 @@
                 at = c * 16 + kind * 8 + t
                 far_mine[at : at + 1, :] = row[:, t * TILE : (t + 1) * TILE]
 
-    pl.semaphore_wait(barrier, (n_seq - 1) + (z_n - 1) + 3)
+    pl.semaphore_wait(barrier, (n_seq - 1) + (z_n - 1) + 4)
 
     def row_copy(i, source, device):
         spot = far_all.at[pl.ds(aligned(source * 32, 32), 32), :]
@@ -196,20 +202,26 @@
         far_row = lax.broadcasted_iota(jnp.int32, (half, rows), 0)
         limit = jnp.minimum(g * n_seq, block - 1)
         for side in range(2):
-            far_block = (2 * (far_row // n_seq) + side) * n_seq + far_row % n_seq
+            chip = far_row // n_seq % 2 * z_n + far_row // (2 * n_seq)
+            far_block = (2 * chip + side) * n_seq + far_row % n_seq
             at = far_at + side * half
             bias[at : at + half, :] = jnp.where(far_block < limit, 0.0, FLOOR)
 
-    def far_slot(which):
-        return pl.ds(aligned(far_at + core * half + which * n_seq, n_seq), n_seq)
+    def far_slot(which_z, which_y, count):
+        at = far_at + core * half + (2 * which_z + which_y) * n_seq
+        return pl.ds(aligned(at, n_seq), count * n_seq)
+
+    def across_copy(which_y):
+        spot = kv.at[:, :, far_slot(zz, which_y, 1), :]
+        return remote(spot, spot, across_send.at[0], across_recv.at[0], across_id)
 
     def far_copy(c, i, which, device):
-        spot = kv.at[c, :, far_slot(which), :]
+        spot = kv.at[c, :, far_slot(which, 0, 2), :]
         return remote(spot, spot, z_send.at[c, i], z_recv.at[c, i], device)
 
     def start_far(c):
         def send(i, carry):
-            far_copy(c, i, zz, (2 * z_peer(i) + core, m)).start()
+            far_copy(c, i, zz, z_id(i)).start()
             return carry
 
         lax.fori_loop(1, z_n, send, 0)
@@ -223,8 +235,8 @@
         for kind in range(2):
             for t in range(tiles):
                 lines = far_all[pl.ds(c * 16 + kind * 8 + t, n_seq, stride=32), :]
-                kv[c, kind, far_slot(zz), t * TILE : (t + 1) * TILE] = lines.astype(BF16)
-    start_far(0)
+                kv[c, kind, far_slot(zz, side_y, 1), t * TILE : (t + 1) * TILE] = lines.astype(BF16)
+    across_copy(side_y).start()
 
     for d in range(1, y_n):
         source = mid_slot(xx * y_n + (yy + y_n - d) % y_n, 1)
@@ -237,7 +249,9 @@
             copy = remote(spot, spot, x_send.at[c, d], x_recv.at[c, d], (g, x_peer(d) * y_n + yy))
             copy.start()
             x_copies.append(copy)
-    start_raw(0, 2, tiles)
+    across_copy(1 - side_y).wait_recv()
+    start_far(0)
+    start_raw(0, 2, 3)
     fill_constants()
 
     def mid_ready(c):
@@ -263,29 +277,40 @@
 
     total = far_at + n_far
 
-    def head_window(j):
-        tile = jnp.maximum((j * depth + depth - 1) // TILE - 1, 0)
-        start = aligned(tile * TILE, TILE)
-        lane = lax.broadcasted_iota(jnp.int32, (8, WINDOW), 1) + start
-        inside = (lane >= j * depth) & (lane < j * depth + depth)
-        keep = jnp.where(inside, 1.0, 0.0)[0:1, :]
-        return pl.ds(start, WINDOW), keep, j * depth - start
-
-    def only(loaded, keep):
-        return (loaded.astype(F32) * keep).astype(BF16)
-
-    def pad_head(u, j, kind, offset):
-        padded[u, kind] = jnp.zeros((WINDOW, rows), BF16)
-        padded[u, kind, pl.ds(aligned(offset, 16), depth), :] = qc_t[
-            kind, pl.ds(aligned(j * depth, depth), depth), :
-        ]
-        return padded[u, kind]
+    wide = PAIR * rows
+
+    def pair_window(i):
+        return aligned(i * PAIR * depth // TILE * TILE, TILE)
+
+    def head_rows(j):
+        return pl.ds(aligned(j * depth, depth), depth)
+
+    def pad_heads(i, kind):
+        padded[kind] = jnp.zeros((WINDOW, wide), BF16)
+        for u in range(PAIR):
+            j = i * PAIR + u
+            at = pl.ds(aligned(j * depth - pair_window(i), 16), depth)
+            padded[kind, at, u * rows : (u + 1) * rows] = qc_t[kind, head_rows(j), :]
+
+    def stacked(loaded, i):
+        lane = lax.broadcasted_iota(jnp.int32, (8, WINDOW), 1) + pair_window(i)
+        heads_of = []
+        for u in range(PAIR):
+            at = (i * PAIR + u) * depth
+            keep = jnp.where((lane >= at) & (lane < at + depth), 1.0, 0.0)[0:1, :]
+            heads_of.append((loaded.astype(F32) * keep).astype(BF16))
+        return jnp.concatenate(heads_of, axis=0)
+
+    def prepare(c, at, size):
+        for kind in range(2):
+            kvt[kind, :, at : at + size] = kv[c, kind, at : at + size, :].T
+
+    def prepare_own(c):
+        for kind in range(2):
+            qc_t[kind] = qc[c, kind].T
+        prepare(c, rows, rows)
 
     def main(c):
-        for kind in range(2):
-            kvt[kind, :, rows:total] = kv[c, kind, rows:total, :].T
-            qc_t[kind] = qc[c, kind].T
-
         def arrive(t):
             key_copy(c, t).wait_recv()
             cols = pl.ds(aligned(t * TILE, TILE), TILE)
@@ -296,61 +321,63 @@
 
         def step(i, carry):
             if c == 0:
-                @pl.when(i == 2)
+                key_copy(1, i).start()
+                query_copy(1, i).start()
+
+                @pl.when(i == 3)
                 def _():
                     forward_far(1)
             else:
-                @pl.when(i == 1)
+                @pl.when(i == 2)
                 def _():
+                    send_far(0, 0)
                     send_far(0, 1)
 
             @pl.when(i == 2)
             def _():
                 core_copy(c, 0).start()
 
-            @pl.when(i == 3)
-            def _():
-                send_far(c, 0)
-
             arrive(i + 1)
-            js = [i * PAIR + u for u in range(PAIR)]
-            windows, queries, cots, cots_t, tops = [], [], [], [], []
-            for u, j in enumerate(js):
-                window, keep, offset = head_window(j)
-                windows.append(window)
-                queries.append(only(qc[c, 0, :, window], keep))
-                cots.append(only(qc[c, 1, :, window], keep))
-                cots_t.append(pad_head(u, j, 1, offset))
-                s = dot(kv[c, 0, :, window], pad_head(u, j, 0, offset)) + bias[...]
-                score[u] = s
-                tops.append(jnp.max(s, axis=0, keepdims=True) * to_log2)
-            inverses, deltas = [], []
-            for u, j in enumerate(js):
-                e = jnp.exp2(score[u] * to_log2 - tops[u])
-                score[u] = e
-                norm = jnp.sum(e, axis=0, keepdims=True)
-                inverse = 1.0 / norm
-                weight[u] = (score[u] * inverse).astype(BF16)
-                inverses.append(inverse)
-                head_rows = pl.ds(aligned(j * depth, depth), depth)
-                mixed = dot(kvt[1, head_rows, :], weight[u]).astype(BF16)
-                out_t[head_rows, :] = mixed
+            window = pl.ds(pair_window(i), WINDOW)
+            pad_heads(i, 0)
+            pad_heads(i, 1)
+            seen = bias[...]
+            s = dot(kv[c, 0, :, window], padded[0]) + jnp.concatenate([seen] * PAIR, axis=1)
+            score[...] = s
+            top = jnp.max(s, axis=0, keepdims=True) * to_log2
+            norm = jnp.zeros((1, wide), F32)
+            for at in range(0, total, rows):
+                e = jnp.exp2(score[at : at + rows, :] * to_log2 - top)
+                score[at : at + rows, :] = e
+                norm = norm + jnp.sum(e, axis=0, keepdims=True)
+            inverse = 1.0 / norm
+            for at in range(0, total, rows):
+                weight[at : at + rows, :] = (score[at : at + rows, :] * inverse).astype(BF16)
+            log_norm = top + jnp.log(norm) * LOG2E
+            deltas = []
+            for u in range(PAIR):
+                j = i * PAIR + u
+                own_cols = slice(u * rows, (u + 1) * rows)
+                mixed = dot(kvt[1, head_rows(j), :], weight[:, own_cols]).astype(BF16)
+                out_t[head_rows(j), :] = mixed
                 delta = jnp.sum(
-                    qc_t[1, head_rows, :].astype(F32) * mixed.astype(F32), axis=0, keepdims=True
+                    qc_t[1, head_rows(j), :].astype(F32) * mixed.astype(F32), axis=0, keepdims=True
                 )
                 deltas.append(delta)
-                stat[c, pl.ds(j, 1), :] = tops[u] + jnp.log(norm) * LOG2E
+                stat[c, pl.ds(j, 1), :] = log_norm[:, own_cols]
                 stat[c, pl.ds(heads + j, 1), :] = delta
-            for u, j in enumerate(js):
-                dprob = dot(kv[c, 1, :, windows[u]], cots_t[u])
-                dscore[u] = (score[u] * ((dprob - deltas[u]) * inverses[u])).astype(BF16)
-                head_rows = pl.ds(aligned(j * depth, depth), depth)
-                dq_t[head_rows, :] = (dot(kvt[0, head_rows, :], dscore[u]) * scale).astype(BF16)
-                for kind, (left, right) in enumerate(((dscore, queries[u]), (weight, cots[u]))):
-                    grad = dot(left[u, rows:total, :], right)
-                    own[c, kind, :, windows[u]] += grad[0:rows]
-                    mid_part[c, kind, :, windows[u]] += grad[rows : rows + mid_rows].astype(BF16)
-                    far_part[c, kind, :, windows[u]] += grad[rows + mid_rows :].astype(BF16)
+            delta = jnp.concatenate(deltas, axis=1)
+            dprob = dot(kv[c, 1, :, window], padded[1])
+            dscore[...] = (score[...] * ((dprob - delta) * inverse)).astype(BF16)
+            for u in range(PAIR):
+                j = i * PAIR + u
+                mixed = dot(kvt[0, head_rows(j), :], dscore[:, u * rows : (u + 1) * rows])
+                dq_t[head_rows(j), :] = (mixed * scale).astype(BF16)
+            for kind, left in enumerate((dscore, weight)):
+                grad = dot(left[rows:total, :], stacked(qc[c, kind, :, window], i))
+                own[c, kind, :, window] += grad[0:rows]
+                mid_part[c, kind, :, window] += grad[rows : rows + mid_rows].astype(BF16)
+                far_part[c, kind, :, window] += grad[rows + mid_rows :].astype(BF16)
             return carry
 
         lax.fori_loop(0, heads // PAIR, step, 0)
@@ -379,9 +406,12 @@
                       (g, xx * y_n + y_peer(d)))
 
     def far_z_copy(c, p, i):
-        src = core_sum.at[c, :, pl.ds(aligned(z_peer(i) * n_seq, n_seq), n_seq), piece(p)]
+        src = core_sum.at[c, :, pl.ds(aligned(z_peer(i) * 2 * n_seq, 2 * n_seq), 2 * n_seq), piece(p)]
         return remote(src, far_in.at[c, i, :, :, piece(p)], fz_send.at[c, p, i], fz_recv.at[c, p, i],
-                      (2 * z_peer(i) + core, m))
+                      z_id(i))
+
+    def cross_copy(c):
+        return remote(cross_out.at[c], cross_in.at[c], cross_send.at[c], cross_recv.at[c], across_id)
 
     def far_row_copy(c, i):
         member = (m + i) % n_seq
@@ -424,19 +454,30 @@
         for d in range(1, y_n):
             mid_y_copy(c, d).start()
 
-    def send_rows(c):
+    def cross_far(c):
         def arrived(i, carry):
             far_z_copy(c, 0, i).wait_recv()
             far_z_copy(c, 1, i).wait_recv()
             return carry
 
         lax.fori_loop(1, z_n, arrived, 0)
-        mine = pl.ds(aligned(zz * n_seq, n_seq), n_seq)
-        for kind in range(2):
-            def add(i, added, kind=kind):
-                return added + far_in[c, i, kind].astype(F32)
-
-            added = lax.fori_loop(1, z_n, add, core_sum[c, kind, mine, :].astype(F32))
+        for which in range(2):
+            at = aligned((2 * zz + which) * n_seq, n_seq)
+            for kind in range(2):
+                def add(i, added, kind=kind, which=which):
+                    return added + far_in[c, i, kind, which * n_seq : (which + 1) * n_seq, :].astype(F32)
+
+                added = core_sum[c, kind, pl.ds(at, n_seq), :].astype(F32)
+                z_sum[which, kind] = lax.fori_loop(1, z_n, add, added)
+        for kind in range(2):
+            cross_out[c, kind] = z_sum[1 - side_y, kind]
+            mine_z[c, kind] = z_sum[side_y, kind]
+        cross_copy(c).start()
+
+    def send_rows(c):
+        cross_copy(c).wait_recv()
+        for kind in range(2):
+            added = mine_z[c, kind] + cross_in[c, kind]
             for t in range(tiles):
                 far_rows[c, pl.ds(kind * 8 + t, n_seq, stride=16), :] = added[:, t * TILE : (t + 1) * TILE]
 
@@ -456,18 +497,19 @@
         there = block < n_blocks - 1
 
         def step(i, carry):
-            for u in range(PAIR):
-                j = i * PAIR + u
-                window, keep, offset = head_window(j)
-                query = only(qn[c, 0, :, window], keep)
-                cot = only(qn[c, 1, :, window], keep)
-                s = dot(kv[c, 0, rows : 2 * rows, window], pad_head(u, j, 0, offset))
-                s = jnp.where(there, s, FLOOR)
-                p = jnp.exp2(s * to_log2 - stat_next[c, pl.ds(j, 1), :])
-                dprob = dot(kv[c, 1, rows : 2 * rows, window], pad_head(u, j, 1, offset))
-                ds = (p * (dprob - stat_next[c, pl.ds(heads + j, 1), :])).astype(BF16)
-                own[c, 0, :, window] += dot(ds, query)
-                own[c, 1, :, window] += dot(p.astype(BF16), cot)
+            window = pl.ds(pair_window(i), WINDOW)
+            pad_heads(i, 0)
+            pad_heads(i, 1)
+            js = [i * PAIR + u for u in range(PAIR)]
+            level = jnp.concatenate([stat_next[c, pl.ds(j, 1), :] for j in js], axis=1)
+            delta = jnp.concatenate([stat_next[c, pl.ds(heads + j, 1), :] for j in js], axis=1)
+            s = dot(kv[c, 0, rows : 2 * rows, window], padded[0])
+            s = jnp.where(there, s, FLOOR)
+            p = jnp.exp2(s * to_log2 - level)
+            dprob = dot(kv[c, 1, rows : 2 * rows, window], padded[1])
+            ds = (p * (dprob - delta)).astype(BF16)
+            own[c, 0, :, window] += dot(ds, stacked(qn[c, 0, :, window], i))
+            own[c, 1, :, window] += dot(p.astype(BF16), stacked(qn[c, 1, :, window], i))
             return carry
 
         lax.fori_loop(0, heads // PAIR, step, 0)
@@ -502,27 +544,38 @@
         store(c, 2, grad_rows.at[c, 0], dk_hbm).start()
         store(c, 3, grad_rows.at[c, 1], dv_hbm).start()
 
+    prepare_own(0)
+    mid_ready(0)
+    prepare(0, mid_at, mid_rows)
     forward_far(0)
     start_far(1)
-    start_raw(1, 0, tiles)
-    mid_ready(0)
+    start_raw(0, 3, tiles)
     far_ready(0)
+    prepare(0, far_at, n_far)
     main(0)
     send_parts(0)
+    start_raw(1, tiles - 1, tiles)
+    prepare_own(1)
     mid_ready(1)
+    prepare(1, mid_at, mid_rows)
     far_ready(1)
+    prepare(1, far_at, n_far)
     main(1)
     send_parts(1)
+    send_far(1, 0)
     send_mid(0)
     send_far(1, 1)
     from_next(0)
-    send_rows(0)
+    cross_far(0)
     send_mid(1)
     from_next(1)
+    send_rows(0)
+    cross_far(1)
     finish(0)
     send_rows(1)
     finish(1)
 
+    across_copy(side_y).wait_send()
     for copy in y_copies + x_copies:
         copy.wait_send()
     for c in range(HALVES):
@@ -531,6 +584,7 @@
             query_copy(c, t).wait_send()
         pair_copy(c).wait_send()
         stat_copy(c).wait_send()
+        cross_copy(c).wait_send()
         core_copy(c, 0).wait_send()
         core_copy(c, 1).wait_send()
         for d in range(1, x_n):
@@ -539,7 +593,7 @@
             mid_y_copy(c, d).wait_send()
 
         def left_z(i, carry, c=c):
-            far_copy(c, i, zz, (2 * z_peer(i) + core, m)).wait_send()
+            far_copy(c, i, zz, z_id(i)).wait_send()
             far_z_copy(c, 0, i).wait_send()
             far_z_copy(c, 1, i).wait_send()
             return carry
@@ -575,7 +629,7 @@
     total = 2 * rows + mid_rows + n_far
     y_n = math.isqrt(n_seq)
     x_n = n_seq // y_n
-    z_n = n_grp // 2
+    z_n = n_grp // 4
     heads = HEADS // HALVES
     tiles = part // TILE
     vmem = pltpu.VMEM
@@ -587,9 +641,9 @@
         vmem((2, part, total), BF16),
         vmem((2, part, rows), BF16),
         vmem((total, rows), F32),
-        vmem((PAIR, total, rows), F32),
-        vmem((PAIR, total, rows), BF16),
-        vmem((PAIR, total, rows), BF16),
+        vmem((total, PAIR * rows), F32),
+        vmem((total, PAIR * rows), BF16),
+        vmem((total, PAIR * rows), BF16),
         vmem((part, rows), BF16),
         vmem((part, rows), BF16),
         vmem((HALVES, 2, rows, part), BF16),
@@ -600,7 +654,7 @@
         vmem((HALVES, 2, n_far, part), BF16),
         vmem((HALVES, 2, half, part), BF16),
         vmem((HALVES, 2, half, part), BF16),
-        vmem((HALVES, z_n, 2, n_seq, part), BF16),
+        vmem((HALVES, z_n, 2, 2 * n_seq, part), BF16),
         vmem((HALVES, n_seq * 16, TILE), F32),
         vmem((HALVES, n_seq * 16, TILE), F32),
         vmem((HALVES, x_n - 1, 2, y_n * coarse, part), BF16),
@@ -609,8 +663,14 @@
         vmem((HALVES, 2, rows, part), BF16),
         vmem((32, TILE), F32),
         vmem((n_seq * 32, TILE), F32),
-        vmem((PAIR, 2, WINDOW, rows), BF16),
+        vmem((2, WINDOW, PAIR * rows), BF16),
+        vmem((HALVES, 2, n_seq, part), F32),
+        vmem((HALVES, 2, n_seq, part), F32),
+        vmem((2, 2, n_seq, part), F32),
+        vmem((HALVES, 2, n_seq, part), F32),
         dma((HALVES * 4,)),
+        dma((1,)), dma((1,)),
+        dma((HALVES,)), dma((HALVES,)),
         dma((n_seq,)), dma((n_seq,)),
         dma((y_n,)), dma((y_n,)),
         dma((HALVES, tiles)), dma((HALVES, tiles)),

time: 146 us -> 144 us (0.986)
  Pallas kernels: 144 us -> 141 us
    pallas_call x1, Pallas kernels: 140 us -> 137 us  [body(): pl.pallas_call(functools.partial(kernel, n_grp, n_seq), out_shape=[jax.Sh...]
where the time goes in v2:
time: 144 us; the launch traced here: 142 us
  Pallas kernels  141 us (98%)
    pallas_call x1, Pallas kernels, body(): pl.pallas_call(functools.partial(kernel, n_grp, n_seq), out_shape=[jax.Sh...  137 us
    pallas_call x1, Pallas kernels, body(): pl.pallas_call(hand_over, grid=(4,), out_shape=[jax.ShapeDtypeStruct((row...  4.02 us

profile of v2, /device:TPU:6, one launch (start us, length us, event | category | flops | bytes accessed | tf_op | source)
XLA Modules:
  0.0 141.9 jit_solution(15493243590763794614)
XLA Ops:
  0.6 137.3 %shard_map.75 = (bf16[256,1280]{1,0:T(8,128)(2,1)}, bf16[256,1280]{1,0:T(8,128)(2,1)}, bf16[256,1280]{1,0:T(8,128)(2,1)}, bf16[256,1280]{1,0:T(8,128)(2,1)}) custom-call(bf16[256,1280]{1,0:T(8,128)(2,1)} %q_hbm.1, bf16[256,1280]{1,0:T(8,128)(2,1)} %k_hbm.1, bf16[256,1280]{1,0:T(8,128)(2,1)} %v_hbm.1, bf16[256,1280]{1,0:T(8,128)(2,1)} %c_hbm.1), custom_call_target="tpu_custom_call" | custom-call | flops 5033164800 | bytes 5242880 | tf_op jit(solution)/shard_map/pallas_call | solution.py:690
  137.9 4.0 %shard_map.76 = (bf16[256,1280]{1,0:T(8,128)(2,1)}, bf16[256,1280]{1,0:T(8,128)(2,1)}, bf16[256,1280]{1,0:T(8,128)(2,1)}, bf16[256,1280]{1,0:T(8,128)(2,1)}) custom-call(bf16[256,1280]{1,0:T(8,128)(2,1)} %get-tuple-element.8.a, bf16[256,1280]{1,0:T(8,128)(2,1)} %get-tuple-element.9.b, bf16[256,1280]{1,0:T(8,128)(2,1)} %get-tuple-element.10.c, ...), custom_call_target="tpu_custom_call" | custom-call | bytes 5242880 | tf_op jit(solution)/shard_map/pallas_call | solution.py:704
